TPU v7x, 32 devices: a whole 2x2x4 slice. The times are simulated.
32 devices in a mesh: parts: 2 (over y), replica: 8 (over z, x), tensor: 2 (over core).
Axes of the slice: x: 2, y: 2, z: 4, core: 2. Of those that a mesh axis runs over, the one named last changes fastest.
Arguments:
- tokens: bfloat16 [2048, 8192], P(('parts', 'replica'), 'tensor'), parts along dimension 0, may hold values from -6 to 6
- base_output: bfloat16 [2048, 8192], P(('parts', 'replica'), 'tensor'), parts along dimension 0, may hold values from -6 to 6
- row_adapter_index: int32 [2048, 1], P(('parts', 'replica')), parts along dimension 0, may hold values from 0 to 7; in each aligned block of 128 rows (0 to 127, 128 to 255, ...) at most 32 rows name the same one
- adapter_table_index: int32 [8], replicated, may hold values from 0 to 7, each once
- adapter_down_table: bfloat16 [8, 8192, 64], P('replica', 'tensor'), may hold values from -0.0625 to 0.0625
- adapter_up_table: bfloat16 [8, 64, 8192], P('replica', None, 'tensor'), may hold values from -0.75 to 0.75
Outputs:
- adapted: bfloat16 [2048, 8192], P(('parts', 'replica'), 'tensor'), parts along dimension 0
There are 2 independent parts, one for each index of `parts`. A program takes and returns all parts, laid end to end along the dimension named above; an argument that names none is the same for every part. Nothing has to cross between parts.
Inputs may be any that keep to these rules, and one draw needn't show every extreme that they name: `row_adapter_index`: within the rows of one replica, at most 32 rows name one adapter; some adapter is named by exactly 32 rows of some replica. `adapter_table_index`: each adapter has its own table index.
All inputs are finite; a program needn't handle non-finite values.
Results may differ from a plain program's by a relative error of at most 0.0056.
Values may be sent and summed in bfloat16 or wider, within the bound.
A program may use at most 64 MiB of HBM per device.

v0:
```python
import jax
import jax.numpy as jnp
from jax import lax
from jax.sharding import PartitionSpec as P

adapter_scale = 2.0


def per_device(
    tokens,
    base_output,
    row_adapter_index,
    adapter_table_index,
    adapter_down_table,
    adapter_up_table,
):
    replicas = lax.axis_size("replica")
    row_count = tokens.shape[0]
    kept_adapter_count = adapter_down_table.shape[0]
    total_adapters = adapter_table_index.shape[0]
    capacity = 2 * row_count // total_adapters
    row_ids = row_adapter_index[:, 0]
    numbers = jnp.arange(total_adapters, dtype=jnp.int32)
    position = jnp.sum(
        jnp.where(row_ids[:, None] == numbers[None, :], adapter_table_index[None, :], 0), axis=1
    )
    owner_rank = position // kept_adapter_count
    local_index = position % kept_adapter_count
    same_adapter = row_ids[:, None] == row_ids[None, :]
    row_numbers = jnp.arange(row_count, dtype=jnp.int32)
    earlier = row_numbers[None, :] < row_numbers[:, None]
    arrival = jnp.sum(jnp.logical_and(same_adapter, earlier).astype(jnp.int32), axis=1)
    destination = (
        owner_rank * (capacity * kept_adapter_count) + arrival * kept_adapter_count + local_index
    )
    slot_count = replicas * capacity * kept_adapter_count
    placing = (destination[None, :] == jnp.arange(slot_count, dtype=jnp.int32)[:, None]).astype(
        jnp.bfloat16
    )
    placing = placing.reshape(replicas, capacity, kept_adapter_count, row_count)
    outgoing = jnp.einsum(
        "scjn,nd->scjd", placing, tokens, preferred_element_type=jnp.float32
    ).astype(jnp.bfloat16)
    partial_value = jnp.einsum(
        "scjd,jdr->scjr",
        lax.all_to_all(outgoing, "replica", split_axis=0, concat_axis=0, tiled=True),
        adapter_down_table,
        preferred_element_type=jnp.float32,
    )
    reduced_activation = lax.psum(partial_value, "tensor").astype(jnp.bfloat16)
    served = jnp.einsum(
        "mqvn,vno->mqvo", reduced_activation, adapter_up_table, preferred_element_type=jnp.float32
    ).astype(jnp.bfloat16)
    returned = lax.all_to_all(served, "replica", split_axis=0, concat_axis=0, tiled=True)
    update_rows = jnp.einsum("scjn,scjd->nd", placing, returned, preferred_element_type=jnp.float32)
    return (base_output.astype(jnp.float32) + adapter_scale * update_rows).astype(jnp.bfloat16)


def solution(mesh):
    placed = (
        P(("parts", "replica"), "tensor"),
        P(("parts", "replica"), "tensor"),
        P(("parts", "replica"), None),
        P(),
        P("replica", "tensor", None),
        P("replica", None, "tensor"),
    )
    return jax.shard_map(
        per_device,
        mesh=mesh,
        in_specs=placed,
        out_specs=P(("parts", "replica"), "tensor"),
        check_vma=False,
    )
```

profile of v0, /device:TPU:0, one launch (start us, length us, event | category | flops | bytes accessed | tf_op | source)
XLA Modules:
  0.0 117.1 jit_solution(5031834787916406448)
XLA Ops:
  0.0 0.0 copy-start
  0.0 0.9 convert_reduce_fusion
  0.9 0.8 select_reduce_fusion
  1.7 0.0 copy-done
  1.7 0.7 fusion.1
  2.5 0.0 copy-start.2
  2.5 55.4 %all_to_all.10 = bf16[8,32,1,4096]{3,1,2,0:T(8,128)(2,1)S(1)} all-to-all(bf16[8,32,1,4096]{3,1,2,0:T(8,128)(2,1)S(1)} %fusion.1), channel_id=1, replica_groups=mesh['parts'=2,'replica'=8,'tensor'=2] {'replica'}, dimensions={0} | all-to-all | bytes 4194304 | tf_op jit(solution)/shard_map/all_to_all | solution.py:46
  57.9 0.0 copy-done.2
  57.9 0.0 copy-start.3
  57.9 0.7 fusion.8
  58.6 3.8 %psum.7 = bf16[8,32,1,64]{3,1,0,2:T(8,128)(2,1)S(1)} all-reduce(f32[8,32,1,64]{3,1,0,2:T(8,128)S(1)} %fusion.8), channel_id=1, replica_groups=mesh['parts'=2,'replica'=8,'tensor'=2] {'tensor'}, use_global_device_ids=true, to_apply=%region_2.3 | all-reduce | flops 16384 | bytes 98304 | tf_op jit(solution)/shard_map/psum | solution.py:50
  62.5 0.0 copy-done.3
  62.5 0.7 fusion
  63.2 0.0 copy-start.1
  63.2 52.2 %all_to_all.11 = bf16[8,32,1,4096]{3,1,2,0:T(8,128)(2,1)S(1)} all-to-all(bf16[8,32,1,4096]{3,1,2,0:T(8,128)(2,1)S(1)} %fusion), channel_id=1, replica_groups=mesh['parts'=2,'replica'=8,'tensor'=2] {'replica'}, dimensions={0} | all-to-all | bytes 4194304 | tf_op jit(solution)/shard_map/all_to_all | solution.py:54
  115.4 0.0 copy-done.1
  115.4 1.7 %fusion.4 = bf16[128,4096]{1,0:T(8,128)(2,1)} fusion(bf16[8,32,1,4096]{3,1,2,0:T(8,128)(2,1)S(1)} %all_to_all.11, bf16[128,4096]{1,0:T(8,128)(2,1)S(1)} %copy-done.1, s32[8,32]{1,0:T(8,128)S(1)} %multiply_add_fusion, s32[128]{0:T(128)S(1)} %multiply_add_fusion.1), kind=kOutput, calls=%fused_computation.7 | convolution fusion | flops 270565376 | bytes 4195840 | tf_op jit(solution)/shard_map/scjn,scjd->nd/dot_general | solution.py:55
  (2 shorter events, 0.0 us)
Async XLA Ops:
  0.0 1.7 %copy-start = (bf16[128,4096]{1,0:T(8,128)(2,1)S(1)}, bf16[128,4096]{1,0:T(8,128)(2,1)}, u32[]{:S(2)}) copy-start(bf16[128,4096]{1,0:T(8,128)(2,1)} %param.6) | copy-start | bytes 3145732
  2.5 55.4 %copy-start.2 = (bf16[1,4096,64]{1,2,0:T(8,128)(2,1)S(1)}, bf16[1,4096,64]{1,2,0:T(8,128)(2,1)}, u32[]{:S(2)}) copy-start(bf16[1,4096,64]{1,2,0:T(8,128)(2,1)} %param.10) | copy-start | bytes 1572868
  57.9 4.6 %copy-start.3 = (bf16[1,64,4096]{2,1,0:T(8,128)(2,1)S(1)}, bf16[1,64,4096]{2,1,0:T(8,128)(2,1)}, u32[]{:S(2)}) copy-start(bf16[1,64,4096]{2,1,0:T(8,128)(2,1)} %param.11) | copy-start | bytes 1572868
  63.2 52.2 %copy-start.1 = (bf16[128,4096]{1,0:T(8,128)(2,1)S(1)}, bf16[128,4096]{1,0:T(8,128)(2,1)}, u32[]{:S(2)}) copy-start(bf16[128,4096]{1,0:T(8,128)(2,1)} %param.7) | copy-start | bytes 3145732
where the time goes:
time: 117 us
  blocking collectives  111 us (95%)
  matrix products  3.81 us (3%)
  other arithmetic  1.7 us (1%)
    all_to_all x1, blocking collectives, per_device(): lax.all_to_all(outgoing, 'replica', split_axis=0, concat_axis=0, tiled=True)  55.4 us
    all_to_all x1, blocking collectives, per_device(): lax.all_to_all(served, 'replica', split_axis=0, concat_axis=0, tiled=True)  52.2 us
    psum x1, blocking collectives, per_device(): reduced_activation = lax.psum(partial_value, 'tensor').astype(jnp.bfloat16)  3.85 us

commit v1 on v0

--- a/solution.py
+++ b/solution.py
@@ -1,12 +1,18 @@
+import functools
+
 import jax
 import jax.numpy as jnp
 from jax import lax
+from jax.experimental import pallas as pl
+from jax.experimental.pallas import tpu as pltpu
 from jax.sharding import PartitionSpec as P
 
 adapter_scale = 2.0
-
-
-def per_device(
+MESH = pl.DeviceIdType.MESH
+COLUMN_CHUNKS = 4
+
+
+def row_exchange(
     tokens,
     base_output,
     row_adapter_index,
@@ -56,6 +62,438 @@
     return (base_output.astype(jnp.float32) + adapter_scale * update_rows).astype(jnp.bfloat16)
 
 
+def flip(value, bit):
+    return 1 - value if bit else value
+
+
+def table_kernel(
+    depth,
+    ids_ref,
+    table_ref,
+    tok,
+    wd,
+    wu,
+    out,
+    xs,
+    pos,
+    down,
+    up,
+    dots,
+    low_part,
+    rs_src,
+    rs_dst,
+    ag,
+    low,
+    expanded,
+    delta,
+    local_sem,
+    x_send,
+    x_recv,
+    pos_send,
+    pos_recv,
+    dx_send,
+    ux_send,
+    dz_send,
+    uz_send,
+    d_recv,
+    u_recv,
+    rs_send,
+    rs_recv,
+    ag_send,
+    ag_recv,
+    back_send,
+    back_recv,
+):
+    rows = tok.shape[0]
+    half = rows // 2
+    quarter = tok.shape[1] // 4
+    chunks, adapters, rank, width = up.shape
+    lanes = 2 * rank
+    part = lax.axis_index("parts")
+    replica = lax.axis_index("replica")
+    core = lax.axis_index("tensor")
+    level, side = replica // 2, replica % 2
+    beside = 2 * level + 1 - side
+
+    def peer(e, other=0):
+        return (flip(part, e >> 1), 2 * level + flip(side, e & 1), flip(core, other))
+
+    def columns(e, offset=0, size=quarter):
+        number = 2 * flip(part, e >> 1) + flip(side, e & 1)
+        return pl.ds(pl.multiple_of(number * quarter + offset, 128), size)
+
+    def remote(src, dst, send, recv, device):
+        return pltpu.make_async_remote_copy(
+            src_ref=src,
+            dst_ref=dst,
+            send_sem=send,
+            recv_sem=recv,
+            device_id=device,
+            device_id_type=MESH,
+        )
+
+    def along(way):
+        return (part, replica + (2 if way else -2), core)
+
+    def can_go(way):
+        return level < depth - 1 if way else level > 0
+
+    def down_z(way, block, own=False):
+        src = wd.at[:, columns(0)] if own else down.at[block]
+        return remote(
+            src, down.at[block], dz_send.at[way, block], d_recv.at[block], along(way)
+        )
+
+    def up_z(way, c, block, own=False):
+        src = wu.at[:, columns(0, c * width, width)] if own else up.at[c, block]
+        return remote(
+            src,
+            up.at[c, block],
+            uz_send.at[way, c, block],
+            u_recv.at[c, block],
+            along(way),
+        )
+
+    def down_x():
+        return remote(wd.at[:, columns(1)], down.at[replica], dx_send.at[0], d_recv.at[replica], peer(1))
+
+    def up_x(c):
+        return remote(
+            wu.at[:, columns(1, c * width, width)],
+            up.at[c, replica],
+            ux_send.at[c],
+            u_recv.at[c, replica],
+            peer(1),
+        )
+
+    def wait_down(block):
+        remote(down.at[block], down.at[block], dx_send.at[0], d_recv.at[block], peer(1)).wait_recv()
+
+    def wait_up(c, block):
+        remote(
+            up.at[c, block], up.at[c, block], ux_send.at[c], u_recv.at[c, block], peer(1)
+        ).wait_recv()
+
+    def token_copy(e):
+        return remote(tok.at[:, columns(e)], xs.at[e], x_send.at[e], x_recv.at[e], peer(e))
+
+    def position_copy(e):
+        return remote(pos.at[0], pos.at[e], pos_send.at[e], pos_recv.at[e], peer(e))
+
+    def scatter_copy(d):
+        return remote(
+            rs_src.at[d], rs_dst.at[d], rs_send.at[d], rs_recv.at[d], peer(d >> 1, d & 1)
+        )
+
+    def gather_copy(d):
+        return remote(ag.at[0], ag.at[d], ag_send.at[d], ag_recv.at[d], peer(d >> 1, d & 1))
+
+    def back_copy(c, e):
+        return remote(
+            delta.at[c, e],
+            out.at[:, columns(0, c * width, width)],
+            back_send.at[c, e],
+            back_recv.at[c, e],
+            peer(e),
+        )
+
+    def back_wait(c, e):
+        remote(
+            delta.at[c, e],
+            out.at[:, columns(e, c * width, width)],
+            back_send.at[c, e],
+            back_recv.at[c, e],
+            peer(e),
+        ).wait_recv()
+
+    barrier = pltpu.get_barrier_semaphore()
+    for d in range(1, 8):
+        pl.semaphore_signal(barrier, inc=1, device_id=peer(d >> 1, d & 1), device_id_type=MESH)
+    for way in (0, 1):
+
+        @pl.when(can_go(way))
+        def _():
+            pl.semaphore_signal(barrier, inc=1, device_id=along(way), device_id_type=MESH)
+
+    own_copies = [
+        pltpu.make_async_copy(wd.at[:, columns(0)], down.at[replica], local_sem.at[0]),
+        pltpu.make_async_copy(tok.at[:, columns(0)], xs.at[0], local_sem.at[1]),
+    ] + [
+        pltpu.make_async_copy(
+            wu.at[:, columns(0, c * width, width)], up.at[c, replica], local_sem.at[2 + c]
+        )
+        for c in range(chunks)
+    ]
+    for copy in own_copies:
+        copy.start()
+    ids = ids_ref[...]
+    position = jnp.zeros_like(ids)
+    for a in range(adapters):
+        position = jnp.where(ids == a, table_ref[a], position)
+    pos[0] = jnp.broadcast_to(position.astype(jnp.float32), (8, rows))
+
+    inner = jnp.logical_and(level > 0, level < depth - 1)
+    pl.semaphore_wait(barrier, 8 + inner.astype(jnp.int32))
+
+    down_x().start()
+    for way in (0, 1):
+
+        @pl.when(can_go(way))
+        def _():
+            down_z(way, replica, own=True).start()
+
+    for c in range(chunks):
+        up_x(c).start()
+    for e in (1, 2, 3):
+        position_copy(e).start()
+    for e in (3, 1, 2):
+        token_copy(e).start()
+    wait_down(beside)
+    for way in (0, 1):
+
+        @pl.when(can_go(way))
+        def _():
+            down_z(way, beside).start()
+
+    def start_own_up():
+        for c in range(chunks):
+            wait_up(c, beside)
+            for way in (0, 1):
+
+                @pl.when(can_go(way))
+                def _():
+                    up_z(way, c, replica, own=True).start()
+                    up_z(way, c, beside).start()
+
+    def arriving(step, wait, forward):
+        for way in (0, 1):
+            source = level - step if way else level + step
+
+            @pl.when(source >= 0 if way else source < depth)
+            def _():
+                for block in (2 * source + side, 2 * source + 1 - side):
+                    wait(block)
+
+                    @pl.when(can_go(way))
+                    def _():
+                        forward(way, block).start()
+
+    pl.when(jnp.logical_not(inner))(start_own_up)
+    for step in range(1, depth):
+        arriving(step, wait_down, down_z)
+    pl.when(inner)(start_own_up)
+
+    for copy in own_copies:
+        copy.wait()
+    for e in (1, 2, 3):
+        position_copy(e).wait_recv()
+        token_copy(e).wait_recv()
+    dots[...] = lax.dot_general(
+        xs[...].reshape(4 * rows, quarter),
+        down[...].reshape(adapters * rank, quarter),
+        (((1,), (1,)), ((), ())),
+        preferred_element_type=jnp.float32,
+    )
+    upper = lax.broadcasted_iota(jnp.int32, (rows, lanes), 1) >= rank
+    first = jnp.logical_not(upper)[: half // 2]
+
+    def place_of(e):
+        place = jnp.transpose(jnp.broadcast_to(pos[e][0:1], (lanes, rows)))
+        return place.astype(jnp.int32) - upper.astype(jnp.int32)
+
+    for e in range(4):
+        place = place_of(e)
+        total = jnp.zeros((rows, lanes), jnp.float32)
+        for g in range(adapters // 2):
+            part_dots = dots[e * rows : (e + 1) * rows, g * lanes : (g + 1) * lanes]
+            total += jnp.where(place == 2 * g, part_dots, 0.0)
+        low_part[e] = total + pltpu.roll(total, rank, 1)
+
+    for d in range(8):
+        start = pl.multiple_of(flip(core, d & 1) * half, half)
+        rs_src[d] = jnp.where(
+            first,
+            low_part[d >> 1, pl.ds(start, half // 2)],
+            low_part[d >> 1, pl.ds(start + half // 2, half // 2)],
+        )
+        if d:
+            scatter_copy(d).start()
+    summed = rs_src[0]
+    for d in range(1, 8):
+        scatter_copy(d).wait_recv()
+        summed += rs_dst[d]
+    ag[0] = summed.astype(jnp.bfloat16)
+    for d in range(1, 8):
+        gather_copy(d).start()
+    for d in range(8):
+        if d:
+            gather_copy(d).wait_recv()
+        packed = ag[d].astype(jnp.float32)
+        rolled = pltpu.roll(packed, rank, 1)
+        start = pl.multiple_of(flip(core, d & 1) * half, half)
+        low[d >> 1, pl.ds(start, half // 2)] = jnp.where(first, packed, rolled)
+        low[d >> 1, pl.ds(start + half // 2, half // 2)] = jnp.where(first, rolled, packed)
+    for e in range(4):
+        place = place_of(e)
+        for g in range(adapters // 2):
+            expanded[e * rows : (e + 1) * rows, g * lanes : (g + 1) * lanes] = jnp.where(
+                place == 2 * g, low[e], 0.0
+            ).astype(jnp.bfloat16)
+
+    for c in range(chunks):
+        for step in range(1, depth):
+            arriving(step, functools.partial(wait_up, c), lambda way, b: up_z(way, c, b))
+        product = jnp.dot(
+            expanded[...],
+            up[c].reshape(adapters * rank, width),
+            preferred_element_type=jnp.float32,
+        ).astype(jnp.bfloat16)
+        delta[c] = product.reshape(4, rows, width)
+        for e in (3, 1, 2):
+            back_copy(c, e).start()
+        pltpu.make_async_copy(
+            delta.at[c, 0], out.at[:, columns(0, c * width, width)], local_sem.at[2 + c]
+        ).start()
+
+    for c in range(chunks):
+        pltpu.make_async_copy(
+            delta.at[c, 0], out.at[:, columns(0, c * width, width)], local_sem.at[2 + c]
+        ).wait()
+        for e in (1, 2, 3):
+            back_wait(c, e)
+            back_copy(c, e).wait_send()
+    down_x().wait_send()
+    for c in range(chunks):
+        up_x(c).wait_send()
+    for e in (1, 2, 3):
+        position_copy(e).wait_send()
+        token_copy(e).wait_send()
+    for d in range(1, 8):
+        scatter_copy(d).wait_send()
+        gather_copy(d).wait_send()
+    for way in (0, 1):
+        for step in range(depth):
+            source = level - step if way else level + step
+            inside = source >= 0 if way else source < depth
+
+            @pl.when(jnp.logical_and(inside, can_go(way)))
+            def _():
+                for block in (2 * source, 2 * source + 1):
+                    down_z(way, block).wait_send()
+                    for c in range(chunks):
+                        up_z(way, c, block).wait_send()
+
+
+def table_gather(
+    tokens,
+    base_output,
+    row_adapter_index,
+    adapter_table_index,
+    adapter_down_table,
+    adapter_up_table,
+):
+    rows, columns = tokens.shape
+    adapters = adapter_table_index.shape[0]
+    rank = adapter_up_table.shape[1]
+    depth = adapters // 2
+    quarter = columns // 4
+    chunks = COLUMN_CHUNKS
+    width = quarter // chunks
+    lanes = 2 * rank
+    half = rows // 2
+    bf16, f32 = jnp.bfloat16, jnp.float32
+    dma = pltpu.SemaphoreType.DMA
+    anywhere = pl.BlockSpec(memory_space=pl.ANY)
+    delta = pl.pallas_call(
+        functools.partial(table_kernel, depth),
+        out_shape=jax.ShapeDtypeStruct((rows, columns), bf16),
+        in_specs=[
+            pl.BlockSpec(memory_space=pltpu.VMEM),
+            pl.BlockSpec(memory_space=pltpu.SMEM),
+            anywhere,
+            anywhere,
+            anywhere,
+        ],
+        out_specs=anywhere,
+        scratch_shapes=[
+            pltpu.VMEM((4, rows, quarter), bf16),
+            pltpu.VMEM((4, 8, rows), f32),
+            pltpu.VMEM((adapters, rank, quarter), bf16),
+            pltpu.VMEM((chunks, adapters, rank, width), bf16),
+            pltpu.VMEM((4 * rows, adapters * rank), f32),
+            pltpu.VMEM((4, rows, lanes), f32),
+            pltpu.VMEM((8, half // 2, lanes), f32),
+            pltpu.VMEM((8, half // 2, lanes), f32),
+            pltpu.VMEM((8, half // 2, lanes), bf16),
+            pltpu.VMEM((4, rows, lanes), f32),
+            pltpu.VMEM((4 * rows, adapters * rank), bf16),
+            pltpu.VMEM((chunks, 4, rows, width), bf16),
+            dma((2 + chunks,)),
+            dma((4,)),
+            dma((4,)),
+            dma((4,)),
+            dma((4,)),
+            dma((1,)),
+            dma((chunks,)),
+            dma((2, adapters)),
+            dma((2, chunks, adapters)),
+            dma((adapters,)),
+            dma((chunks, adapters)),
+            dma((8,)),
+            dma((8,)),
+            dma((8,)),
+            dma((8,)),
+            dma((chunks, 4)),
+            dma((chunks, 4)),
+        ],
+        compiler_params=pltpu.CompilerParams(
+            collective_id=0, has_side_effects=True, vmem_limit_bytes=40 * 1024 * 1024
+        ),
+    )(
+        row_adapter_index.reshape(1, rows),
+        adapter_table_index,
+        tokens,
+        adapter_down_table[0].T,
+        adapter_up_table[0],
+    )
+    return (
+        base_output.astype(jnp.float32) + adapter_scale * delta.astype(jnp.float32)
+    ).astype(jnp.bfloat16)
+
+
+def per_device(
+    tokens,
+    base_output,
+    row_adapter_index,
+    adapter_table_index,
+    adapter_down_table,
+    adapter_up_table,
+):
+    replicas = lax.axis_size("replica")
+    rows, columns = tokens.shape
+    kept, _, rank = adapter_down_table.shape
+    tables = 2 * replicas * kept * rank * columns // 4
+    slots = 2 * (2 * rows) * columns
+    planes = (
+        lax.axis_size("parts") == 2
+        and lax.axis_size("tensor") == 2
+        and replicas % 2 == 0
+        and kept == 1
+        and rows == 128
+        and rank == 64
+        and columns % (4 * COLUMN_CHUNKS * 128) == 0
+    )
+    plan = table_gather if planes and tables <= slots else row_exchange
+    return plan(
+        tokens,
+        base_output,
+        row_adapter_index,
+        adapter_table_index,
+        adapter_down_table,
+        adapter_up_table,
+    )
+
+
 def solution(mesh):
     placed = (
         P(("parts", "replica"), "tensor"),

time: 117 us -> 61.9 us (0.53)
  blocking collectives: 111 us -> 0 us
  Pallas kernels: 0 us -> 55.8 us
  local copies, waits for them, and re-layouts: 0.02 us -> 4.62 us
  matrix products: 3.81 us -> 0 us
    all_to_all x2 -> x0, blocking collectives: 108 us -> none  [the longest x1 55.4 us: per_device(): lax.all_to_all(outgoing, 'replica', split_axis=0, concat_axis=0, tiled=True)]
    pallas_call x0 -> x1, Pallas kernels: none -> 55.8 us  [table_gather(): pl.pallas_call(functools.partial(table_kernel, depth), out_shape=jax.Shap...]
    unnamed x8 -> x12, local copies, waits for them, and re-layouts: 0.02 us -> 4.62 us
    psum x1 -> x0, blocking collectives: 3.85 us -> none  [per_device(): reduced_activation = lax.psum(partial_value, 'tensor').astype(jnp.bfloat16)]
    dot_general x4 -> x0, matrix products: 3.81 us -> none  [the longest x1 1.69 us: per_device(): jnp.einsum('scjn,scjd->nd', placing, returned, preferred_element_type=jnp...]
    reduce_sum x2 -> x0, other arithmetic: 1.69 us -> none  [the longest x1 0.93 us: per_device(): jnp.sum(jnp.logical_and(same_adapter, earlier).astype(jnp.int32), axis=1)]
    convert_element_type x0 -> x1, other arithmetic: none -> 1.28 us  [table_gather(): return (base_output.astype(jnp.float32) + adapter_scale * delta.astype(jn...]
where the time goes in v1:
time: 61.9 us; the launch traced here: 61.7 us
  Pallas kernels  55.8 us (90%)
  local copies, waits for them, and re-layouts  4.62 us (7%)
  other arithmetic  1.28 us (2%)
    pallas_call x1, Pallas kernels, table_gather(): pl.pallas_call(functools.partial(table_kernel, depth), out_shape=jax.Shap...  55.8 us
    unnamed x12, local copies, waits for them, and re-layouts  4.62 us
    convert_element_type x1, other arithmetic, table_gather(): return (base_output.astype(jnp.float32) + adapter_scale * delta.astype(jn...  1.28 us

profile of v1, /device:TPU:0, one launch (start us, length us, event | category | flops | bytes accessed | tf_op | source)
XLA Modules:
  0.0 61.7 jit_solution(3601102222510814979)
XLA Ops:
  0.0 0.0 copy-start
  0.0 1.2 %copy-done = bf16[128,4096]{1,0:T(8,128)(2,1)S(1)} copy-done((bf16[128,4096]{1,0:T(8,128)(2,1)S(1)}, bf16[128,4096]{1,0:T(8,128)(2,1)}, u32[]{:S(2)}) %copy-start) | copy-done | bytes 1048600
  1.2 0.0 copy-start.1
  1.2 1.0 %copy-done.1 = bf16[1,4096,64]{1,2,0:T(8,128)(2,1)S(1)} copy-done((bf16[1,4096,64]{1,2,0:T(8,128)(2,1)S(1)}, bf16[1,4096,64]{1,2,0:T(8,128)(2,1)}, u32[]{:S(2)}) %copy-start.1) | copy-done | bytes 524312
  2.3 0.0 copy-start.2
  2.3 1.0 %copy-done.2 = bf16[1,64,4096]{2,1,0:T(8,128)(2,1)S(1)} copy-done((bf16[1,64,4096]{2,1,0:T(8,128)(2,1)S(1)}, bf16[1,64,4096]{2,1,0:T(8,128)(2,1)}, u32[]{:S(2)}) %copy-start.2) | copy-done | bytes 524312
  3.3 0.0 copy-start.3
  3.3 0.7 %copy-done.3 = s32[128,1]{0,1:T(1,128)S(1)} copy-done((s32[128,1]{0,1:T(1,128)S(1)}, s32[128,1]{0,1:T(1,128)}, u32[]{:S(2)}) %copy-start.3) | copy-done | bytes 536
  4.0 0.0 copy-start.4
  4.0 0.7 %copy-done.4 = s32[8]{0:T(128)S(1)} copy-done((s32[8]{0:T(128)S(1)}, s32[8]{0:T(128)}, u32[]{:S(2)}) %copy-start.4) | copy-done | bytes 56
  4.6 0.0 copy-start.5
  4.6 55.8 %shard_map.64 = bf16[128,4096]{1,0:T(8,128)(2,1)S(1)} custom-call(s32[1,128]{1,0:T(1,128)S(1)} %bitcast.7, s32[8]{0:T(128)S(1)} %copy-done.4, bf16[128,4096]{1,0:T(8,128)(2,1)S(1)} %copy-done, bf16[64,4096]{1,0:T(8,128)(2,1)S(1)} %bitcast.5, bf16[64,4096]{1,0:T(8,128)(2,1)S(1)} %bitcast.6), custom_call_target="tpu_custom_call" | custom-call | tf_op jit(solution)/shard_map/pallas_call | solution.py:407
  60.4 0.0 copy-done.5
  60.4 1.3 %add_convert_fusion = bf16[128,4096]{1,0:T(8,128)(2,1)} fusion(bf16[128,4096]{1,0:T(8,128)(2,1)S(1)} %shard_map.64, bf16[128,4096]{1,0:T(8,128)(2,1)S(1)} %copy-done.5), kind=kLoop, calls=%fused_computation | loop fusion | flops 2621440 | bytes 3145728 | tf_op jit(solution)/shard_map/convert_element_type | solution.py:461
Async XLA Ops:
  0.0 1.2 %copy-start = (bf16[128,4096]{1,0:T(8,128)(2,1)S(1)}, bf16[128,4096]{1,0:T(8,128)(2,1)}, u32[]{:S(2)}) copy-start(bf16[128,4096]{1,0:T(8,128)(2,1)} %tok.1) | copy-start | bytes 3145732
  1.2 1.0 %copy-start.1 = (bf16[1,4096,64]{1,2,0:T(8,128)(2,1)S(1)}, bf16[1,4096,64]{1,2,0:T(8,128)(2,1)}, u32[]{:S(2)}) copy-start(bf16[1,4096,64]{1,2,0:T(8,128)(2,1)} %param.10) | copy-start | bytes 1572868
  2.3 1.0 %copy-start.2 = (bf16[1,64,4096]{2,1,0:T(8,128)(2,1)S(1)}, bf16[1,64,4096]{2,1,0:T(8,128)(2,1)}, u32[]{:S(2)}) copy-start(bf16[1,64,4096]{2,1,0:T(8,128)(2,1)} %param.11) | copy-start | bytes 1572868
  3.3 0.7 %copy-start.3 = (s32[128,1]{0,1:T(1,128)S(1)}, s32[128,1]{0,1:T(1,128)}, u32[]{:S(2)}) copy-start(s32[128,1]{0,1:T(1,128)} %param.8) | copy-start | bytes 1540
  4.0 0.7 %copy-start.4 = (s32[8]{0:T(128)S(1)}, s32[8]{0:T(128)}, u32[]{:S(2)}) copy-start(s32[8]{0:T(128)} %table_ref.1) | copy-start | bytes 100
  4.6 55.8 %copy-start.5 = (bf16[128,4096]{1,0:T(8,128)(2,1)S(1)}, bf16[128,4096]{1,0:T(8,128)(2,1)}, u32[]{:S(2)}) copy-start(bf16[128,4096]{1,0:T(8,128)(2,1)} %param.7) | copy-start | bytes 3145732

commit v2 on v1

--- a/solution.py
+++ b/solution.py
@@ -9,7 +9,7 @@
 
 adapter_scale = 2.0
 MESH = pl.DeviceIdType.MESH
-COLUMN_CHUNKS = 4
+CHUNK_EIGHTHS = (3, 3, 2)
 
 
 def row_exchange(
@@ -68,6 +68,7 @@
 
 def table_kernel(
     depth,
+    widths,
     ids_ref,
     table_ref,
     tok,
@@ -77,15 +78,12 @@
     xs,
     pos,
     down,
-    up,
     dots,
-    low_part,
     rs_src,
     rs_dst,
     ag,
     low,
     expanded,
-    delta,
     local_sem,
     x_send,
     x_recv,
@@ -93,9 +91,10 @@
     pos_recv,
     dx_send,
     ux_send,
+    ux_recv,
     dz_send,
+    d_recv,
     uz_send,
-    d_recv,
     u_recv,
     rs_send,
     rs_recv,
@@ -103,11 +102,15 @@
     ag_recv,
     back_send,
     back_recv,
+    *buffers,
 ):
+    chunks = len(widths)
+    starts = [sum(widths[:c]) for c in range(chunks)]
+    up, delta = buffers[:chunks], buffers[chunks:]
     rows = tok.shape[0]
     half = rows // 2
     quarter = tok.shape[1] // 4
-    chunks, adapters, rank, width = up.shape
+    adapters, rank, _ = down.shape
     lanes = 2 * rank
     part = lax.axis_index("parts")
     replica = lax.axis_index("replica")
@@ -121,6 +124,12 @@
     def columns(e, offset=0, size=quarter):
         number = 2 * flip(part, e >> 1) + flip(side, e & 1)
         return pl.ds(pl.multiple_of(number * quarter + offset, 128), size)
+
+    def chunk(e, c):
+        return columns(e, starts[c], widths[c])
+
+    def pair(source):
+        return pl.ds(2 * source, 2)
 
     def remote(src, dst, send, recv, device):
         return pltpu.make_async_remote_copy(
@@ -140,39 +149,33 @@
 
     def down_z(way, block, own=False):
         src = wd.at[:, columns(0)] if own else down.at[block]
+        return remote(src, down.at[block], dz_send.at[way, block], d_recv.at[block], along(way))
+
+    def up_z(way, c, source):
+        both = up[c].at[pair(source)]
+        return remote(both, both, uz_send.at[way, c, source], u_recv.at[c, source], along(way))
+
+    def down_x():
         return remote(
-            src, down.at[block], dz_send.at[way, block], d_recv.at[block], along(way)
+            wd.at[:, columns(1)], down.at[replica], dx_send.at[0], d_recv.at[replica], peer(1)
         )
-
-    def up_z(way, c, block, own=False):
-        src = wu.at[:, columns(0, c * width, width)] if own else up.at[c, block]
-        return remote(
-            src,
-            up.at[c, block],
-            uz_send.at[way, c, block],
-            u_recv.at[c, block],
-            along(way),
-        )
-
-    def down_x():
-        return remote(wd.at[:, columns(1)], down.at[replica], dx_send.at[0], d_recv.at[replica], peer(1))
 
     def up_x(c):
         return remote(
-            wu.at[:, columns(1, c * width, width)],
-            up.at[c, replica],
-            ux_send.at[c],
-            u_recv.at[c, replica],
-            peer(1),
+            wu.at[:, chunk(1, c)], up[c].at[replica], ux_send.at[c], ux_recv.at[c], peer(1)
         )
 
     def wait_down(block):
-        remote(down.at[block], down.at[block], dx_send.at[0], d_recv.at[block], peer(1)).wait_recv()
-
-    def wait_up(c, block):
-        remote(
-            up.at[c, block], up.at[c, block], ux_send.at[c], u_recv.at[c, block], peer(1)
-        ).wait_recv()
+        there = down.at[block]
+        remote(there, there, dx_send.at[0], d_recv.at[block], peer(1)).wait_recv()
+
+    def wait_up(c, source):
+        both = up[c].at[pair(source)]
+        remote(both, both, ux_send.at[c], u_recv.at[c, source], peer(1)).wait_recv()
+
+    def wait_up_x(c):
+        there = up[c].at[beside]
+        remote(there, there, ux_send.at[c], ux_recv.at[c], peer(1)).wait_recv()
 
     def token_copy(e):
         return remote(tok.at[:, columns(e)], xs.at[e], x_send.at[e], x_recv.at[e], peer(e))
@@ -180,31 +183,26 @@
     def position_copy(e):
         return remote(pos.at[0], pos.at[e], pos_send.at[e], pos_recv.at[e], peer(e))
 
-    def scatter_copy(d):
-        return remote(
-            rs_src.at[d], rs_dst.at[d], rs_send.at[d], rs_recv.at[d], peer(d >> 1, d & 1)
-        )
+    def scatter_copy(e, other):
+        d = 2 * e + other
+        src = rs_src.at[e, flip(core, other)]
+        return remote(src, rs_dst.at[d], rs_send.at[d], rs_recv.at[d], peer(e, other))
 
     def gather_copy(d):
         return remote(ag.at[0], ag.at[d], ag_send.at[d], ag_recv.at[d], peer(d >> 1, d & 1))
 
     def back_copy(c, e):
         return remote(
-            delta.at[c, e],
-            out.at[:, columns(0, c * width, width)],
-            back_send.at[c, e],
-            back_recv.at[c, e],
-            peer(e),
+            delta[c].at[e], out.at[:, chunk(0, c)], back_send.at[c, e], back_recv.at[c, e], peer(e)
         )
 
     def back_wait(c, e):
         remote(
-            delta.at[c, e],
-            out.at[:, columns(e, c * width, width)],
-            back_send.at[c, e],
-            back_recv.at[c, e],
-            peer(e),
+            delta[c].at[e], out.at[:, chunk(e, c)], back_send.at[c, e], back_recv.at[c, e], peer(e)
         ).wait_recv()
+
+    def own_back(c):
+        return pltpu.make_async_copy(delta[c].at[0], out.at[:, chunk(0, c)], local_sem.at[2 + c])
 
     barrier = pltpu.get_barrier_semaphore()
     for d in range(1, 8):
@@ -215,16 +213,15 @@
         def _():
             pl.semaphore_signal(barrier, inc=1, device_id=along(way), device_id_type=MESH)
 
-    own_copies = [
+    own_up = [
+        pltpu.make_async_copy(wu.at[:, chunk(0, c)], up[c].at[replica], local_sem.at[2 + c])
+        for c in range(chunks)
+    ]
+    own_down = [
         pltpu.make_async_copy(wd.at[:, columns(0)], down.at[replica], local_sem.at[0]),
         pltpu.make_async_copy(tok.at[:, columns(0)], xs.at[0], local_sem.at[1]),
-    ] + [
-        pltpu.make_async_copy(
-            wu.at[:, columns(0, c * width, width)], up.at[c, replica], local_sem.at[2 + c]
-        )
-        for c in range(chunks)
     ]
-    for copy in own_copies:
+    for copy in own_up + own_down:
         copy.start()
     ids = ids_ref[...]
     position = jnp.zeros_like(ids)
@@ -242,12 +239,12 @@
         def _():
             down_z(way, replica, own=True).start()
 
+    for e in (3, 1, 2):
+        token_copy(e).start()
+    for e in (1, 2, 3):
+        position_copy(e).start()
     for c in range(chunks):
         up_x(c).start()
-    for e in (1, 2, 3):
-        position_copy(e).start()
-    for e in (3, 1, 2):
-        token_copy(e).start()
     wait_down(beside)
     for way in (0, 1):
 
@@ -255,15 +252,17 @@
         def _():
             down_z(way, beside).start()
 
+    for copy in own_up:
+        copy.wait()
+
     def start_own_up():
         for c in range(chunks):
-            wait_up(c, beside)
+            wait_up_x(c)
             for way in (0, 1):
 
                 @pl.when(can_go(way))
                 def _():
-                    up_z(way, c, replica, own=True).start()
-                    up_z(way, c, beside).start()
+                    up_z(way, c, level).start()
 
     def arriving(step, wait, forward):
         for way in (0, 1):
@@ -271,19 +270,27 @@
 
             @pl.when(source >= 0 if way else source < depth)
             def _():
-                for block in (2 * source + side, 2 * source + 1 - side):
-                    wait(block)
-
-                    @pl.when(can_go(way))
-                    def _():
-                        forward(way, block).start()
+                wait(source)
+
+                @pl.when(can_go(way))
+                def _():
+                    forward(way, source).start()
+
+    def arriving_up(c, steps=range(1, depth)):
+        for step in steps:
+            arriving(step, functools.partial(wait_up, c), lambda way, s: up_z(way, c, s))
 
     pl.when(jnp.logical_not(inner))(start_own_up)
     for step in range(1, depth):
-        arriving(step, wait_down, down_z)
+        for toward in (side, 1 - side):
+            arriving(
+                step,
+                lambda source: wait_down(2 * source + toward),
+                lambda way, source: down_z(way, 2 * source + toward),
+            )
     pl.when(inner)(start_own_up)
 
-    for copy in own_copies:
+    for copy in own_down:
         copy.wait()
     for e in (1, 2, 3):
         position_copy(e).wait_recv()
@@ -301,30 +308,37 @@
         place = jnp.transpose(jnp.broadcast_to(pos[e][0:1], (lanes, rows)))
         return place.astype(jnp.int32) - upper.astype(jnp.int32)
 
-    for e in range(4):
+    for e in (3, 1, 2, 0):
         place = place_of(e)
         total = jnp.zeros((rows, lanes), jnp.float32)
         for g in range(adapters // 2):
             part_dots = dots[e * rows : (e + 1) * rows, g * lanes : (g + 1) * lanes]
             total += jnp.where(place == 2 * g, part_dots, 0.0)
-        low_part[e] = total + pltpu.roll(total, rank, 1)
-
-    for d in range(8):
-        start = pl.multiple_of(flip(core, d & 1) * half, half)
-        rs_src[d] = jnp.where(
-            first,
-            low_part[d >> 1, pl.ds(start, half // 2)],
-            low_part[d >> 1, pl.ds(start + half // 2, half // 2)],
-        )
-        if d:
-            scatter_copy(d).start()
-    summed = rs_src[0]
+        total += pltpu.roll(total, rank, 1)
+        for h in (0, 1):
+            lower = total[h * half : h * half + half // 2]
+            higher = total[h * half + half // 2 : (h + 1) * half]
+            rs_src[e, h] = jnp.where(first, lower, higher)
+        for other in (1, 0):
+            if e or other:
+                scatter_copy(e, other).start()
+
+    @pl.when(inner)
+    def _():
+        arriving_up(0, (1,))
+
+    summed = rs_src[0, core]
     for d in range(1, 8):
-        scatter_copy(d).wait_recv()
+        scatter_copy(d >> 1, d & 1).wait_recv()
         summed += rs_dst[d]
     ag[0] = summed.astype(jnp.bfloat16)
-    for d in range(1, 8):
+    for d in (7, 6, 3, 2, 5, 4, 1):
         gather_copy(d).start()
+
+    @pl.when(inner)
+    def _():
+        arriving_up(0, range(2, depth))
+
     for d in range(8):
         if d:
             gather_copy(d).wait_recv()
@@ -341,36 +355,29 @@
             ).astype(jnp.bfloat16)
 
     for c in range(chunks):
-        for step in range(1, depth):
-            arriving(step, functools.partial(wait_up, c), lambda way, b: up_z(way, c, b))
+        if c:
+            arriving_up(c)
+        else:
+            pl.when(jnp.logical_not(inner))(functools.partial(arriving_up, c))
         product = jnp.dot(
             expanded[...],
-            up[c].reshape(adapters * rank, width),
+            up[c][...].reshape(adapters * rank, widths[c]),
             preferred_element_type=jnp.float32,
         ).astype(jnp.bfloat16)
-        delta[c] = product.reshape(4, rows, width)
+        delta[c][...] = product.reshape(4, rows, widths[c])
         for e in (3, 1, 2):
             back_copy(c, e).start()
-        pltpu.make_async_copy(
-            delta.at[c, 0], out.at[:, columns(0, c * width, width)], local_sem.at[2 + c]
-        ).start()
-
-    for c in range(chunks):
-        pltpu.make_async_copy(
-            delta.at[c, 0], out.at[:, columns(0, c * width, width)], local_sem.at[2 + c]
-        ).wait()
-        for e in (1, 2, 3):
-            back_wait(c, e)
-            back_copy(c, e).wait_send()
+        own_back(c).start()
+
     down_x().wait_send()
+    for d in range(1, 8):
+        scatter_copy(d >> 1, d & 1).wait_send()
+        gather_copy(d).wait_send()
     for c in range(chunks):
         up_x(c).wait_send()
     for e in (1, 2, 3):
         position_copy(e).wait_send()
         token_copy(e).wait_send()
-    for d in range(1, 8):
-        scatter_copy(d).wait_send()
-        gather_copy(d).wait_send()
     for way in (0, 1):
         for step in range(depth):
             source = level - step if way else level + step
@@ -378,10 +385,16 @@
 
             @pl.when(jnp.logical_and(inside, can_go(way)))
             def _():
-                for block in (2 * source, 2 * source + 1):
-                    down_z(way, block).wait_send()
-                    for c in range(chunks):
-                        up_z(way, c, block).wait_send()
+                down_z(way, 2 * source).wait_send()
+                down_z(way, 2 * source + 1).wait_send()
+                for c in range(chunks):
+                    up_z(way, c, source).wait_send()
+
+    for c in range(chunks):
+        own_back(c).wait()
+        for e in (1, 2, 3):
+            back_wait(c, e)
+            back_copy(c, e).wait_send()
 
 
 def table_gather(
@@ -397,15 +410,15 @@
     rank = adapter_up_table.shape[1]
     depth = adapters // 2
     quarter = columns // 4
-    chunks = COLUMN_CHUNKS
-    width = quarter // chunks
+    widths = tuple(quarter * share // 8 for share in CHUNK_EIGHTHS)
+    chunks = len(widths)
     lanes = 2 * rank
     half = rows // 2
     bf16, f32 = jnp.bfloat16, jnp.float32
     dma = pltpu.SemaphoreType.DMA
     anywhere = pl.BlockSpec(memory_space=pl.ANY)
     delta = pl.pallas_call(
-        functools.partial(table_kernel, depth),
+        functools.partial(table_kernel, depth, widths),
         out_shape=jax.ShapeDtypeStruct((rows, columns), bf16),
         in_specs=[
             pl.BlockSpec(memory_space=pltpu.VMEM),
@@ -419,15 +432,12 @@
             pltpu.VMEM((4, rows, quarter), bf16),
             pltpu.VMEM((4, 8, rows), f32),
             pltpu.VMEM((adapters, rank, quarter), bf16),
-            pltpu.VMEM((chunks, adapters, rank, width), bf16),
             pltpu.VMEM((4 * rows, adapters * rank), f32),
-            pltpu.VMEM((4, rows, lanes), f32),
-            pltpu.VMEM((8, half // 2, lanes), f32),
+            pltpu.VMEM((4, 2, half // 2, lanes), f32),
             pltpu.VMEM((8, half // 2, lanes), f32),
             pltpu.VMEM((8, half // 2, lanes), bf16),
             pltpu.VMEM((4, rows, lanes), f32),
             pltpu.VMEM((4 * rows, adapters * rank), bf16),
-            pltpu.VMEM((chunks, 4, rows, width), bf16),
             dma((2 + chunks,)),
             dma((4,)),
             dma((4,)),
@@ -435,19 +445,22 @@
             dma((4,)),
             dma((1,)),
             dma((chunks,)),
+            dma((chunks,)),
             dma((2, adapters)),
-            dma((2, chunks, adapters)),
             dma((adapters,)),
-            dma((chunks, adapters)),
+            dma((2, chunks, depth)),
+            dma((chunks, depth)),
             dma((8,)),
             dma((8,)),
             dma((8,)),
             dma((8,)),
             dma((chunks, 4)),
             dma((chunks, 4)),
+            *[pltpu.VMEM((adapters, rank, width), bf16) for width in widths],
+            *[pltpu.VMEM((4, rows, width), bf16) for width in widths],
         ],
         compiler_params=pltpu.CompilerParams(
-            collective_id=0, has_side_effects=True, vmem_limit_bytes=40 * 1024 * 1024
+            collective_id=0, has_side_effects=True, vmem_limit_bytes=60 * 1024 * 1024
         ),
     )(
         row_adapter_index.reshape(1, rows),
@@ -481,7 +494,7 @@
         and kept == 1
         and rows == 128
         and rank == 64
-        and columns % (4 * COLUMN_CHUNKS * 128) == 0
+        and columns % (4 * 8 * 128) == 0
     )
     plan = table_gather if planes and tables <= slots else row_exchange
     return plan(

time: 61.9 us -> 53.8 us (0.87)
  local copies, waits for them, and re-layouts: 4.62 us -> 0.01 us
  Pallas kernels: 55.8 us -> 51.2 us
  other arithmetic: 1.28 us -> 2.51 us
    unnamed x12 -> x2, local copies, waits for them, and re-layouts: 4.62 us -> 0.01 us
    pallas_call x1, Pallas kernels: 55.8 us -> 51.2 us  [table_gather(): pl.pallas_call(functools.partial(table_kernel, depth, widths), out_shape=...]
    convert_element_type x1, other arithmetic: 1.28 us -> 2.51 us  [table_gather(): return (base_output.astype(jnp.float32) + adapter_scale * delta.astype(jn...]
where the time goes in v2:
time: 53.8 us; the launch traced here: 53.7 us
  Pallas kernels  51.2 us (95%)
  other arithmetic  2.51 us (5%)
    pallas_call x1, Pallas kernels, table_gather(): pl.pallas_call(functools.partial(table_kernel, depth, widths), out_shape=...  51.2 us
    convert_element_type x1, other arithmetic, table_gather(): return (base_output.astype(jnp.float32) + adapter_scale * delta.astype(jn...  2.51 us

profile of v2, /device:TPU:0, one launch (start us, length us, event | category | flops | bytes accessed | tf_op | source)
XLA Modules:
  0.0 53.7 jit_solution(17244338848603696291)
XLA Ops:
  0.0 0.0 copy-start
  0.0 51.2 %shard_map.64 = bf16[128,4096]{1,0:T(8,128)(2,1)} custom-call(s32[1,128]{1,0:T(1,128)} %bitcast.7, s32[8]{0:T(128)} %table_ref.1, bf16[128,4096]{1,0:T(8,128)(2,1)} %tok.1, bf16[64,4096]{1,0:T(8,128)(2,1)} %bitcast.5, bf16[64,4096]{1,0:T(8,128)(2,1)} %bitcast.6), custom_call_target="tpu_custom_call" | custom-call | tf_op jit(solution)/shard_map/pallas_call | solution.py:420
  51.2 0.0 copy-done
  51.2 2.5 %add_convert_fusion = bf16[128,4096]{1,0:T(8,128)(2,1)} fusion(bf16[128,4096]{1,0:T(8,128)(2,1)} %shard_map.64, bf16[128,4096]{1,0:T(8,128)(2,1)S(1)} %copy-done), kind=kLoop, calls=%fused_computation | loop fusion | flops 2621440 | bytes 3145728 | tf_op jit(solution)/shard_map/convert_element_type | solution.py:474
Async XLA Ops:
  0.0 51.2 %copy-start = (bf16[128,4096]{1,0:T(8,128)(2,1)S(1)}, bf16[128,4096]{1,0:T(8,128)(2,1)}, u32[]{:S(2)}) copy-start(bf16[128,4096]{1,0:T(8,128)(2,1)} %param.7) | copy-start | bytes 3145732

commit v3 on v2

--- a/solution.py
+++ b/solution.py
@@ -9,7 +9,7 @@
 
 adapter_scale = 2.0
 MESH = pl.DeviceIdType.MESH
-CHUNK_EIGHTHS = (3, 3, 2)
+CHUNK_EIGHTHS = (3, 2, 2, 1)
 
 
 def row_exchange(
@@ -69,8 +69,8 @@
 def table_kernel(
     depth,
     widths,
-    ids_ref,
-    table_ref,
+    ids_hbm,
+    table_hbm,
     tok,
     wd,
     wu,
@@ -102,6 +102,8 @@
     ag_recv,
     back_send,
     back_recv,
+    ids_ref,
+    table_ref,
     *buffers,
 ):
     chunks = len(widths)
@@ -221,8 +223,14 @@
         pltpu.make_async_copy(wd.at[:, columns(0)], down.at[replica], local_sem.at[0]),
         pltpu.make_async_copy(tok.at[:, columns(0)], xs.at[0], local_sem.at[1]),
     ]
-    for copy in own_up + own_down:
+    indices = [
+        pltpu.make_async_copy(ids_hbm, ids_ref, local_sem.at[2 + chunks]),
+        pltpu.make_async_copy(table_hbm, table_ref, local_sem.at[3 + chunks]),
+    ]
+    for copy in indices + own_up + own_down:
         copy.start()
+    for copy in indices:
+        copy.wait()
     ids = ids_ref[...]
     position = jnp.zeros_like(ids)
     for a in range(adapters):
@@ -255,8 +263,8 @@
     for copy in own_up:
         copy.wait()
 
-    def start_own_up():
-        for c in range(chunks):
+    def start_own_up(numbers):
+        for c in numbers:
             wait_up_x(c)
             for way in (0, 1):
 
@@ -280,7 +288,13 @@
         for step in steps:
             arriving(step, functools.partial(wait_up, c), lambda way, s: up_z(way, c, s))
 
-    pl.when(jnp.logical_not(inner))(start_own_up)
+    def pass_ahead(c):
+        if c < chunks:
+            arriving_up(c, range(2, depth))
+        if c + 1 < chunks:
+            arriving_up(c + 1, (1,))
+
+    pl.when(jnp.logical_not(inner))(functools.partial(start_own_up, range(chunks)))
     for step in range(1, depth):
         for toward in (side, 1 - side):
             arriving(
@@ -288,7 +302,7 @@
                 lambda source: wait_down(2 * source + toward),
                 lambda way, source: down_z(way, 2 * source + toward),
             )
-    pl.when(inner)(start_own_up)
+    pl.when(inner)(functools.partial(start_own_up, (0,)))
 
     for copy in own_down:
         copy.wait()
@@ -326,6 +340,7 @@
     @pl.when(inner)
     def _():
         arriving_up(0, (1,))
+        start_own_up(range(1, chunks))
 
     summed = rs_src[0, core]
     for d in range(1, 8):
@@ -335,9 +350,7 @@
     for d in (7, 6, 3, 2, 5, 4, 1):
         gather_copy(d).start()
 
-    @pl.when(inner)
-    def _():
-        arriving_up(0, range(2, depth))
+    pl.when(inner)(functools.partial(pass_ahead, 0))
 
     for d in range(8):
         if d:
@@ -355,10 +368,8 @@
             ).astype(jnp.bfloat16)
 
     for c in range(chunks):
-        if c:
-            arriving_up(c)
-        else:
-            pl.when(jnp.logical_not(inner))(functools.partial(arriving_up, c))
+        pl.when(jnp.logical_not(inner))(functools.partial(arriving_up, c))
+        pl.when(inner)(functools.partial(pass_ahead, c + 1))
         product = jnp.dot(
             expanded[...],
             up[c][...].reshape(adapters * rank, widths[c]),
@@ -421,8 +432,8 @@
         functools.partial(table_kernel, depth, widths),
         out_shape=jax.ShapeDtypeStruct((rows, columns), bf16),
         in_specs=[
-            pl.BlockSpec(memory_space=pltpu.VMEM),
-            pl.BlockSpec(memory_space=pltpu.SMEM),
+            anywhere,
+            anywhere,
             anywhere,
             anywhere,
             anywhere,
@@ -438,7 +449,7 @@
             pltpu.VMEM((8, half // 2, lanes), bf16),
             pltpu.VMEM((4, rows, lanes), f32),
             pltpu.VMEM((4 * rows, adapters * rank), bf16),
-            dma((2 + chunks,)),
+            dma((4 + chunks,)),
             dma((4,)),
             dma((4,)),
             dma((4,)),
@@ -456,18 +467,25 @@
             dma((8,)),
             dma((chunks, 4)),
             dma((chunks, 4)),
+            pltpu.VMEM((1, rows), jnp.int32),
+            pltpu.SMEM((adapters,), jnp.int32),
             *[pltpu.VMEM((adapters, rank, width), bf16) for width in widths],
             *[pltpu.VMEM((4, rows, width), bf16) for width in widths],
         ],
         compiler_params=pltpu.CompilerParams(
-            collective_id=0, has_side_effects=True, vmem_limit_bytes=60 * 1024 * 1024
+            collective_id=0, has_side_effects=True, vmem_limit_bytes=40 * 1024 * 1024
         ),
     )(
-        row_adapter_index.reshape(1, rows),
-        adapter_table_index,
-        tokens,
-        adapter_down_table[0].T,
-        adapter_up_table[0],
+        *[
+            pltpu.with_memory_space_constraint(operand, pltpu.HBM)
+            for operand in (
+                row_adapter_index.reshape(1, rows),
+                adapter_table_index,
+                tokens,
+                adapter_down_table[0].T,
+                adapter_up_table[0],
+            )
+        ]
     )
     return (
         base_output.astype(jnp.float32) + adapter_scale * delta.astype(jnp.float32)

time: 53.8 us -> 50.7 us (0.942)
  Pallas kernels: 51.2 us -> 49.3 us
  other arithmetic: 2.51 us -> 1.28 us
    pallas_call x1, Pallas kernels: 51.2 us -> 49.3 us  [table_gather(): pl.pallas_call(functools.partial(table_kernel, depth, widths), out_shape=...]
    convert_element_type x1, other arithmetic: 2.51 us -> 1.28 us  [table_gather(): return (base_output.astype(jnp.float32) + adapter_scale * delta.astype(jn...]
where the time goes in v3:
time: 50.7 us; the launch traced here: 50.6 us
  Pallas kernels  49.3 us (97%)
  other arithmetic  1.28 us (3%)
    pallas_call x1, Pallas kernels, table_gather(): pl.pallas_call(functools.partial(table_kernel, depth, widths), out_shape=...  49.3 us
    convert_element_type x1, other arithmetic, table_gather(): return (base_output.astype(jnp.float32) + adapter_scale * delta.astype(jn...  1.28 us

profile of v3, /device:TPU:0, one launch (start us, length us, event | category | flops | bytes accessed | tf_op | source)
XLA Modules:
  0.0 50.6 jit_solution(9432688372854976021)
XLA Ops:
  0.0 0.0 copy-start
  0.0 49.3 %shard_map.64 = bf16[128,4096]{1,0:T(8,128)(2,1)S(1)} custom-call(s32[1,128]{1,0:T(1,128)} %bitcast.7, s32[8]{0:T(128)} %table_hbm.1, bf16[128,4096]{1,0:T(8,128)(2,1)} %tok.1, bf16[64,4096]{1,0:T(8,128)(2,1)} %bitcast.5, bf16[64,4096]{1,0:T(8,128)(2,1)} %bitcast.6), custom_call_target="tpu_custom_call" | custom-call | tf_op jit(solution)/shard_map/pallas_call | solution.py:431
  49.3 0.0 copy-done
  49.3 1.3 %add_convert_fusion = bf16[128,4096]{1,0:T(8,128)(2,1)} fusion(bf16[128,4096]{1,0:T(8,128)(2,1)S(1)} %shard_map.64, bf16[128,4096]{1,0:T(8,128)(2,1)S(1)} %copy-done), kind=kLoop, calls=%fused_computation | loop fusion | flops 2621440 | bytes 3145728 | tf_op jit(solution)/shard_map/convert_element_type | solution.py:492
Async XLA Ops:
  0.0 49.3 %copy-start = (bf16[128,4096]{1,0:T(8,128)(2,1)S(1)}, bf16[128,4096]{1,0:T(8,128)(2,1)}, u32[]{:S(2)}) copy-start(bf16[128,4096]{1,0:T(8,128)(2,1)} %param.7) | copy-start | bytes 3145732

commit v4 on v3

--- a/solution.py
+++ b/solution.py
@@ -104,6 +104,7 @@
     back_recv,
     ids_ref,
     table_ref,
+    place_of,
     *buffers,
 ):
     chunks = len(widths)
@@ -295,35 +296,39 @@
             arriving_up(c + 1, (1,))
 
     pl.when(jnp.logical_not(inner))(functools.partial(start_own_up, range(chunks)))
-    for step in range(1, depth):
+    def arriving_down(step):
         for toward in (side, 1 - side):
             arriving(
                 step,
                 lambda source: wait_down(2 * source + toward),
                 lambda way, source: down_z(way, 2 * source + toward),
             )
+
+    for step in range(1, depth - 1):
+        arriving_down(step)
     pl.when(inner)(functools.partial(start_own_up, (0,)))
 
+    upper = lax.broadcasted_iota(jnp.int32, (rows, lanes), 1) >= rank
+    first = jnp.logical_not(upper)[: half // 2]
     for copy in own_down:
         copy.wait()
+    for e in range(4):
+        if e:
+            position_copy(e).wait_recv()
+        spread = jnp.transpose(jnp.broadcast_to(pos[e][0:1], (lanes, rows)))
+        place_of[e] = spread.astype(jnp.int32) - upper.astype(jnp.int32)
     for e in (1, 2, 3):
-        position_copy(e).wait_recv()
         token_copy(e).wait_recv()
+    arriving_down(depth - 1)
+
     dots[...] = lax.dot_general(
         xs[...].reshape(4 * rows, quarter),
         down[...].reshape(adapters * rank, quarter),
         (((1,), (1,)), ((), ())),
         preferred_element_type=jnp.float32,
     )
-    upper = lax.broadcasted_iota(jnp.int32, (rows, lanes), 1) >= rank
-    first = jnp.logical_not(upper)[: half // 2]
-
-    def place_of(e):
-        place = jnp.transpose(jnp.broadcast_to(pos[e][0:1], (lanes, rows)))
-        return place.astype(jnp.int32) - upper.astype(jnp.int32)
-
     for e in (3, 1, 2, 0):
-        place = place_of(e)
+        place = place_of[e]
         total = jnp.zeros((rows, lanes), jnp.float32)
         for g in range(adapters // 2):
             part_dots = dots[e * rows : (e + 1) * rows, g * lanes : (g + 1) * lanes]
@@ -352,22 +357,32 @@
 
     pl.when(inner)(functools.partial(pass_ahead, 0))
 
-    for d in range(8):
-        if d:
-            gather_copy(d).wait_recv()
-        packed = ag[d].astype(jnp.float32)
-        rolled = pltpu.roll(packed, rank, 1)
-        start = pl.multiple_of(flip(core, d & 1) * half, half)
-        low[d >> 1, pl.ds(start, half // 2)] = jnp.where(first, packed, rolled)
-        low[d >> 1, pl.ds(start + half // 2, half // 2)] = jnp.where(first, rolled, packed)
-    for e in range(4):
-        place = place_of(e)
+    pl.when(jnp.logical_not(inner))(functools.partial(arriving_up, 0))
+    for e in (3, 1, 2, 0):
+        for d in (2 * e, 2 * e + 1):
+            if d:
+                gather_copy(d).wait_recv()
+            packed = ag[d].astype(jnp.float32)
+            rolled = pltpu.roll(packed, rank, 1)
+            start = pl.multiple_of(flip(core, d & 1) * half, half)
+            low[e, pl.ds(start, half // 2)] = jnp.where(first, packed, rolled)
+            low[e, pl.ds(start + half // 2, half // 2)] = jnp.where(first, rolled, packed)
+        place = place_of[e]
         for g in range(adapters // 2):
             expanded[e * rows : (e + 1) * rows, g * lanes : (g + 1) * lanes] = jnp.where(
                 place == 2 * g, low[e], 0.0
             ).astype(jnp.bfloat16)
-
-    for c in range(chunks):
+        delta[0][e] = jnp.dot(
+            expanded[e * rows : (e + 1) * rows],
+            up[0][...].reshape(adapters * rank, widths[0]),
+            preferred_element_type=jnp.float32,
+        ).astype(jnp.bfloat16)
+        if e:
+            back_copy(0, e).start()
+    own_back(0).start()
+    pl.when(inner)(functools.partial(pass_ahead, 1))
+
+    for c in range(1, chunks):
         pl.when(jnp.logical_not(inner))(functools.partial(arriving_up, c))
         pl.when(inner)(functools.partial(pass_ahead, c + 1))
         product = jnp.dot(
@@ -469,6 +484,7 @@
             dma((chunks, 4)),
             pltpu.VMEM((1, rows), jnp.int32),
             pltpu.SMEM((adapters,), jnp.int32),
+            pltpu.VMEM((4, rows, lanes), jnp.int32),
             *[pltpu.VMEM((adapters, rank, width), bf16) for width in widths],
             *[pltpu.VMEM((4, rows, width), bf16) for width in widths],
         ],

time: 50.7 us -> 50.7 us (level)
  no operation moved by 1% of the time
where the time goes in v4:
time: 50.7 us; the launch traced here: 50.6 us
  Pallas kernels  49.3 us (97%)
  other arithmetic  1.28 us (3%)
    pallas_call x1, Pallas kernels, table_gather(): pl.pallas_call(functools.partial(table_kernel, depth, widths), out_shape=...  49.3 us
    convert_element_type x1, other arithmetic, table_gather(): return (base_output.astype(jnp.float32) + adapter_scale * delta.astype(jn...  1.28 us

profile of v4, /device:TPU:0, one launch (start us, length us, event | category | flops | bytes accessed | tf_op | source)
XLA Modules:
  0.0 50.6 jit_solution(11505936665156429696)
XLA Ops:
  0.0 0.0 copy-start
  0.0 49.3 %shard_map.64 = bf16[128,4096]{1,0:T(8,128)(2,1)S(1)} custom-call(s32[1,128]{1,0:T(1,128)} %bitcast.7, s32[8]{0:T(128)} %table_hbm.1, bf16[128,4096]{1,0:T(8,128)(2,1)} %tok.1, bf16[64,4096]{1,0:T(8,128)(2,1)} %bitcast.5, bf16[64,4096]{1,0:T(8,128)(2,1)} %bitcast.6), custom_call_target="tpu_custom_call" | custom-call | tf_op jit(solution)/shard_map/pallas_call | solution.py:446
  49.3 0.0 copy-done
  49.3 1.3 %add_convert_fusion = bf16[128,4096]{1,0:T(8,128)(2,1)} fusion(bf16[128,4096]{1,0:T(8,128)(2,1)S(1)} %shard_map.64, bf16[128,4096]{1,0:T(8,128)(2,1)S(1)} %copy-done), kind=kLoop, calls=%fused_computation | loop fusion | flops 2621440 | bytes 3145728 | tf_op jit(solution)/shard_map/convert_element_type | solution.py:508
Async XLA Ops:
  0.0 49.3 %copy-start = (bf16[128,4096]{1,0:T(8,128)(2,1)S(1)}, bf16[128,4096]{1,0:T(8,128)(2,1)}, u32[]{:S(2)}) copy-start(bf16[128,4096]{1,0:T(8,128)(2,1)} %param.7) | copy-start | bytes 3145732

commit v5 on v3

--- a/solution.py
+++ b/solution.py
@@ -247,12 +247,16 @@
         def _():
             down_z(way, replica, own=True).start()
 
+    def start_up_x():
+        for c in range(chunks):
+            up_x(c).start()
+
+    pl.when(jnp.logical_not(inner))(start_up_x)
     for e in (3, 1, 2):
         token_copy(e).start()
     for e in (1, 2, 3):
         position_copy(e).start()
-    for c in range(chunks):
-        up_x(c).start()
+    pl.when(inner)(start_up_x)
     wait_down(beside)
     for way in (0, 1):
 

time: 50.7 us -> 51 us (level)
  no operation moved by 1% of the time
where the time goes in v5:
time: 51 us; the launch traced here: 50.8 us
  Pallas kernels  49.5 us (97%)
  other arithmetic  1.28 us (3%)
    pallas_call x1, Pallas kernels, table_gather(): pl.pallas_call(functools.partial(table_kernel, depth, widths), out_shape=...  49.5 us
    convert_element_type x1, other arithmetic, table_gather(): return (base_output.astype(jnp.float32) + adapter_scale * delta.astype(jn...  1.28 us

profile of v5, /device:TPU:0, one launch (start us, length us, event | category | flops | bytes accessed | tf_op | source)
XLA Modules:
  0.0 50.8 jit_solution(9693861188532314508)
XLA Ops:
  0.0 0.0 copy-start
  0.0 49.5 %shard_map.64 = bf16[128,4096]{1,0:T(8,128)(2,1)S(1)} custom-call(s32[1,128]{1,0:T(1,128)} %bitcast.7, s32[8]{0:T(128)} %table_hbm.1, bf16[128,4096]{1,0:T(8,128)(2,1)} %tok.1, bf16[64,4096]{1,0:T(8,128)(2,1)} %bitcast.5, bf16[64,4096]{1,0:T(8,128)(2,1)} %bitcast.6), custom_call_target="tpu_custom_call" | custom-call | tf_op jit(solution)/shard_map/pallas_call | solution.py:435
  49.6 0.0 copy-done
  49.6 1.3 %add_convert_fusion = bf16[128,4096]{1,0:T(8,128)(2,1)} fusion(bf16[128,4096]{1,0:T(8,128)(2,1)S(1)} %shard_map.64, bf16[128,4096]{1,0:T(8,128)(2,1)S(1)} %copy-done), kind=kLoop, calls=%fused_computation | loop fusion | flops 2621440 | bytes 3145728 | tf_op jit(solution)/shard_map/convert_element_type | solution.py:496
Async XLA Ops:
  0.0 49.6 %copy-start = (bf16[128,4096]{1,0:T(8,128)(2,1)S(1)}, bf16[128,4096]{1,0:T(8,128)(2,1)}, u32[]{:S(2)}) copy-start(bf16[128,4096]{1,0:T(8,128)(2,1)} %param.7) | copy-start | bytes 3145732
